TPU v7x, 128 devices: a whole 4x4x4 slice. The times are simulated.
128 devices in a mesh: section: 4 (over y), tensor: 32 (over z, x, core).
Axes of the slice: x: 4, y: 4, z: 4, core: 2. Of those that a mesh axis runs over, the one named last changes fastest.
Arguments:
- token_ids: int32 [4, 128], replicated, may hold values from 0 to 64127
- embedding: bfloat16 [64128, 8192], P('section', 'tensor'), may hold values from -6 to 6
- norm_gain: float32 [4, 8192], P('section'), may hold values from 0.1 to 1.9
- query_weight: bfloat16 [4, 8192, 8192], P('section', None, 'tensor'), may hold values from -0.0625 to 0.0625
- keyval_weight: bfloat16 [4, 8192, 2048], P('section', None, 'tensor'), may hold values from -0.0625 to 0.0625
- output_weight: bfloat16 [4, 8192, 8192], P('section', 'tensor'), may hold values from -0.0625 to 0.0625
- prefix_cache: bfloat16 [4, 128, 128, 2, 1024], P('section', 'tensor')
- prefix_lengths: int32 [128], P('tensor'), may hold values from 16 to 128, as said below
Outputs:
- answers: float32 [4, 128, 8192], P('section', 'tensor')
Inputs may be any that keep to these rules, and one draw needn't show every extreme that they name: `prefix_lengths`: some row has exactly 128 live positions.
All inputs are finite; a program needn't handle non-finite values.
Results may differ from a plain program's by a relative error of at most 0.039.
Values may be sent and summed in bfloat16 or wider, within the bound.
No kernel may reach another device: no remote copies, remote signals or barrier semaphores. Data moves between devices by JAX's collectives and lax.ppermute only.
A program may use at most 128 MiB of HBM per device.

v0:
```python
import jax
import jax.numpy as jnp
from jax import lax
from jax.sharding import PartitionSpec as P

HEADS = 64
KVH = 8
HD = 128
NORM_EPSILON = 1e-05
ROPE_BASE = 500000.0


def passed_along(block, axis, distance):
    devices = range(lax.axis_size(axis))
    route = [(i - distance, i) for i in devices if i - distance in devices]
    return lax.ppermute(block, axis, route)


def rope_tables(positions, head_dim):
    half_dim = head_dim // 2
    frequency = ROPE_BASE ** (-(jnp.arange(half_dim, dtype=jnp.float32) * 2.0 / head_dim))
    angles = positions.astype(jnp.float32)[:, None] * frequency[None, :]
    cosine = jnp.concatenate([jnp.cos(angles), jnp.cos(angles)], axis=-1)
    sine_table = jnp.concatenate([jnp.sin(angles), jnp.sin(angles)], axis=-1)
    return (cosine, sine_table)


def rotate(vectors, cosine, sine_table):
    half_dim = vectors.shape[-1] // 2
    swapped = jnp.concatenate([-vectors[..., half_dim:], vectors[..., :half_dim]], axis=-1)
    return vectors * cosine[:, None, :] + swapped * sine_table[:, None, :]


def normalize(values, gain_vec):
    scaling = lax.rsqrt(jnp.mean(values * values, axis=-1, keepdims=True) + NORM_EPSILON)
    return (values * scaling * gain_vec).astype(jnp.bfloat16)


def attend(queries, prefix, fresh_rows, live_len, step_index):
    row_count, kv_heads, group_size, head_dim = queries.shape
    step_total = fresh_rows.shape[0]
    past_keys = prefix[:, :, 0, :].reshape(row_count, -1, kv_heads, head_dim)
    past_vals = prefix[:, :, 1, :].reshape(row_count, -1, kv_heads, head_dim)
    new_keys = fresh_rows[:, :, 0, :].reshape(step_total, row_count, kv_heads, head_dim)
    new_vals = fresh_rows[:, :, 1, :].reshape(step_total, row_count, kv_heads, head_dim)
    score_scale = head_dim ** (-0.5)
    past_score = (
        jnp.einsum("rkgd,rlkd->rkgl", queries, past_keys, preferred_element_type=jnp.float32)
        * score_scale
    )
    new_score = (
        jnp.einsum("rkgd,srkd->rkgs", queries, new_keys, preferred_element_type=jnp.float32)
        * score_scale
    )
    past_mask = jnp.arange(past_keys.shape[1])[None, None, None, :] < live_len[:, None, None, None]
    new_mask = jnp.arange(step_total)[None, None, None, :] <= step_index
    past_score = jnp.where(past_mask, past_score, -1e30)
    new_score = jnp.where(new_mask, new_score, -1e30)
    top_score = jnp.maximum(jnp.max(past_score, axis=-1), jnp.max(new_score, axis=-1))[..., None]
    past_weight = jnp.exp(past_score - top_score)
    new_weight = jnp.exp(new_score - top_score)
    weight_total = jnp.sum(past_weight, axis=-1, keepdims=True) + jnp.sum(
        new_weight, axis=-1, keepdims=True
    )
    past_prob = (past_weight / weight_total).astype(jnp.bfloat16)
    new_prob = (new_weight / weight_total).astype(jnp.bfloat16)
    attended = jnp.einsum(
        "rkgl,rlkd->rkgd", past_prob, past_vals, preferred_element_type=jnp.float32
    )
    attended = attended + jnp.einsum(
        "rkgs,srkd->rkgd", new_prob, new_vals, preferred_element_type=jnp.float32
    )
    return attended.astype(jnp.bfloat16).reshape(row_count, kv_heads * group_size * head_dim)


def body(
    token_ids,
    embedding,
    norm_gain,
    query_weight,
    keyval_weight,
    output_weight,
    prefix_cache,
    prefix_lengths,
):
    n_tensor = lax.axis_size("tensor")
    section_pos = lax.axis_index("section")
    tensor_pos = lax.axis_index("tensor")
    last_section = lax.axis_size("section") - 1
    step_count = token_ids.shape[0]
    vocab_part = embedding.shape[0]
    own_rows = prefix_lengths.shape[0]
    model_width = embedding.shape[1] * n_tensor
    kv_width = KVH * HD
    group_size = HEADS // KVH
    local_ids = token_ids - section_pos * vocab_part
    inside = (local_ids >= 0) & (local_ids < vocab_part)
    picked = jnp.take(embedding, jnp.clip(local_ids, 0, vocab_part - 1), axis=0)
    partial_embed = jnp.where(inside[:, :, None], picked.astype(jnp.float32), 0.0)
    columns = lax.psum(partial_embed.astype(jnp.bfloat16), "section")
    own_embed = lax.all_to_all(columns, "tensor", split_axis=1, concat_axis=2, tiled=True)
    block_count = 1
    block_rows = own_rows // block_count
    item_count = step_count * block_count
    tick_count = item_count + last_section
    gain_vec = norm_gain[0]
    query_mat = query_weight[0]
    keyval_mat = keyval_weight[0]
    output_mat = output_weight[0]
    cache_rows = prefix_cache[0]
    carried = jnp.zeros((block_rows, model_width), jnp.float32)
    fresh_kv = jnp.zeros((step_count, own_rows, 2, kv_width), jnp.bfloat16)
    finals = jnp.zeros((step_count, own_rows, model_width), jnp.float32)

    def advance(tick_index, carry_state):
        incoming, fresh_kv, finals = carry_state
        item_index = tick_index - section_pos
        is_valid = (item_index >= 0) & (item_index < item_count)
        item_index = jnp.clip(item_index, 0, item_count - 1)
        step_index = item_index // block_count
        row_start = item_index % block_count * block_rows
        step_embed = lax.dynamic_index_in_dim(own_embed, step_index, 0, keepdims=False)
        first_input = step_embed.astype(jnp.float32)
        hidden_in = jnp.where(section_pos == 0, first_input, incoming)
        normed = lax.all_gather(normalize(hidden_in, gain_vec), "tensor", axis=0, tiled=True)
        queries = jnp.dot(normed, query_mat, preferred_element_type=jnp.float32)
        keyvals = jnp.dot(normed, keyval_mat, preferred_element_type=jnp.float32)
        queries, keyvals = (
            lax.all_to_all(queries, "tensor", split_axis=0, concat_axis=1, tiled=True),
            lax.all_to_all(keyvals, "tensor", split_axis=0, concat_axis=1, tiled=True),
        )
        cosine, sine_table = rope_tables(prefix_lengths + step_index, HD)
        turned_q = rotate(queries.reshape(block_rows, HEADS, HD), cosine, sine_table).astype(
            jnp.bfloat16
        )
        turned_k = rotate(
            keyvals[:, :kv_width].reshape(block_rows, KVH, HD), cosine, sine_table
        ).astype(jnp.bfloat16)
        value_cols = keyvals[:, kv_width:].astype(jnp.bfloat16)
        entry_kv = jnp.stack([turned_k.reshape(block_rows, kv_width), value_cols], axis=1)
        current = lax.dynamic_slice(
            fresh_kv, (step_index, row_start, 0, 0), (1, block_rows, 2, kv_width)
        )
        fresh_kv = lax.dynamic_update_slice(
            fresh_kv, jnp.where(is_valid, entry_kv[None], current), (step_index, row_start, 0, 0)
        )
        mixed_out = attend(
            turned_q.reshape(block_rows, KVH, group_size, HD),
            cache_rows,
            fresh_kv,
            prefix_lengths,
            step_index,
        )
        head_cols = lax.all_to_all(mixed_out, "tensor", split_axis=1, concat_axis=0, tiled=True)
        partial_value = (
            jnp.dot(head_cols, output_mat, preferred_element_type=jnp.float32)
            .astype(jnp.bfloat16)
            .astype(jnp.float32)
        )
        summed_all = lax.psum(partial_value.astype(jnp.bfloat16), "tensor").astype(jnp.float32)
        summed = lax.dynamic_slice_in_dim(summed_all, tensor_pos * block_rows, block_rows, 0)
        hidden_out = hidden_in + summed
        write_final = is_valid & (section_pos == last_section)
        current_final = lax.dynamic_slice(
            finals, (step_index, row_start, 0), (1, block_rows, model_width)
        )
        finals = lax.dynamic_update_slice(
            finals,
            jnp.where(write_final, hidden_out[None], current_final),
            (step_index, row_start, 0),
        )
        outgoing = passed_along(hidden_out, "section", 1)
        return (outgoing, fresh_kv, finals)

    spent, fresh_kv, finals = lax.fori_loop(0, tick_count, advance, (carried, fresh_kv, finals))
    answers = lax.psum_scatter(finals, "section", scatter_dimension=0, tiled=True)
    return answers


def solution(mesh):
    in_specs = (
        P(),
        P("section", "tensor"),
        P("section", None),
        P("section", None, "tensor"),
        P("section", None, "tensor"),
        P("section", "tensor", None),
        P("section", "tensor", None, None, None),
        P("tensor"),
    )
    out_specs = P("section", "tensor", None)
    return jax.shard_map(body, mesh=mesh, in_specs=in_specs, out_specs=out_specs, check_vma=False)
```

profile of v0, /device:TPU:0, one launch (start us, length us, event | category | flops | bytes accessed | tf_op | source)
XLA Modules:
  0.0 1589.0 jit_solution(3336385134684504714)
XLA Ops:
  15.2 44.3 %all-reduce.5.cloned.1.call-done = bf16[4,128,256]{2,0,1:T(4,128)(2,1)} async-done(((bf16[4,128,256]{2,0,1:T(4,128)(2,1)}), bf16[4,128,256]{2,0,1:T(4,128)(2,1)}) %all-reduce.5.cloned.1.call-update) | async-done | bytes 262160 | tf_op jit(solution)/shard_map/psum | solution.py:100
  76.9 1456.6 %while.19 = (s32[]{:T(128)}, f32[4,8192]{1,0:T(4,128)S(1)}, bf16[4,4,2,1024]{3,1,2,0:T(4,128)(2,1)S(1)}, f32[4,4,8192]{2,1,0:T(4,128)}, pred[]{:T(512)}, /*index...) while((s32[]{:T(128)}, f32[4,8192]{1,0:T(4,128)S(1)}, ...), condition=%wide.region_8.9_spmd, body=%wide.region_1.8_spmd.sunk | while | flops 1228397952 | bytes 74761704 | solution.py:175
  81.3 41.5 %all-gather.5.cloned.1.call-done = bf16[32,4,8192]{2,1,0:T(4,128)(2,1)} async-done(((bf16[1,4,8192]{2,1,0:T(4,128)(2,1)}), bf16[32,4,8192]{2,1,0:T(4,128)(2,1)}) %all-gather.5.cloned.1.call-update) | async-done | bytes 2097168 | tf_op jit(solution)/shard_map/while/body/eval_jaxpr/all_gather | solution.py:125
  155.0 11.0 all_to_all.139
  170.3 105.2 %all-reduce.9.cloned.1.call-done = bf16[128,8192]{1,0:T(8,128)(2,1)} async-done(((bf16[128,8192]{1,0:T(8,128)(2,1)}), bf16[128,8192]{1,0:T(8,128)(2,1)}) %all-reduce.9.cloned.1.call-update) | async-done | bytes 2097168 | tf_op jit(solution)/shard_map/while/body/eval_jaxpr/psum | solution.py:160
  287.8 43.3 %all-gather.5.cloned.1.call-done = bf16[32,4,8192]{2,1,0:T(4,128)(2,1)} async-done(((bf16[1,4,8192]{2,1,0:T(4,128)(2,1)}), bf16[32,4,8192]{2,1,0:T(4,128)(2,1)}) %all-gather.5.cloned.1.call-update) | async-done | bytes 2097168 | tf_op jit(solution)/shard_map/while/body/eval_jaxpr/all_gather | solution.py:125
  363.3 11.0 all_to_all.139
  378.6 105.2 %all-reduce.9.cloned.1.call-done = bf16[128,8192]{1,0:T(8,128)(2,1)} async-done(((bf16[128,8192]{1,0:T(8,128)(2,1)}), bf16[128,8192]{1,0:T(8,128)(2,1)}) %all-reduce.9.cloned.1.call-update) | async-done | bytes 2097168 | tf_op jit(solution)/shard_map/while/body/eval_jaxpr/psum | solution.py:160
  496.1 43.3 %all-gather.5.cloned.1.call-done = bf16[32,4,8192]{2,1,0:T(4,128)(2,1)} async-done(((bf16[1,4,8192]{2,1,0:T(4,128)(2,1)}), bf16[32,4,8192]{2,1,0:T(4,128)(2,1)}) %all-gather.5.cloned.1.call-update) | async-done | bytes 2097168 | tf_op jit(solution)/shard_map/while/body/eval_jaxpr/all_gather | solution.py:125
  571.6 11.0 all_to_all.139
  586.9 105.2 %all-reduce.9.cloned.1.call-done = bf16[128,8192]{1,0:T(8,128)(2,1)} async-done(((bf16[128,8192]{1,0:T(8,128)(2,1)}), bf16[128,8192]{1,0:T(8,128)(2,1)}) %all-reduce.9.cloned.1.call-update) | async-done | bytes 2097168 | tf_op jit(solution)/shard_map/while/body/eval_jaxpr/psum | solution.py:160
  704.4 43.7 %all-gather.5.cloned.1.call-done = bf16[32,4,8192]{2,1,0:T(4,128)(2,1)} async-done(((bf16[1,4,8192]{2,1,0:T(4,128)(2,1)}), bf16[32,4,8192]{2,1,0:T(4,128)(2,1)}) %all-gather.5.cloned.1.call-update) | async-done | bytes 2097168 | tf_op jit(solution)/shard_map/while/body/eval_jaxpr/all_gather | solution.py:125
  780.2 11.0 all_to_all.139
  795.5 105.2 %all-reduce.9.cloned.1.call-done = bf16[128,8192]{1,0:T(8,128)(2,1)} async-done(((bf16[128,8192]{1,0:T(8,128)(2,1)}), bf16[128,8192]{1,0:T(8,128)(2,1)}) %all-reduce.9.cloned.1.call-update) | async-done | bytes 2097168 | tf_op jit(solution)/shard_map/while/body/eval_jaxpr/psum | solution.py:160
  913.0 43.4 %all-gather.5.cloned.1.call-done = bf16[32,4,8192]{2,1,0:T(4,128)(2,1)} async-done(((bf16[1,4,8192]{2,1,0:T(4,128)(2,1)}), bf16[32,4,8192]{2,1,0:T(4,128)(2,1)}) %all-gather.5.cloned.1.call-update) | async-done | bytes 2097168 | tf_op jit(solution)/shard_map/while/body/eval_jaxpr/all_gather | solution.py:125
  988.5 11.0 all_to_all.139
  1003.8 105.2 %all-reduce.9.cloned.1.call-done = bf16[128,8192]{1,0:T(8,128)(2,1)} async-done(((bf16[128,8192]{1,0:T(8,128)(2,1)}), bf16[128,8192]{1,0:T(8,128)(2,1)}) %all-reduce.9.cloned.1.call-update) | async-done | bytes 2097168 | tf_op jit(solution)/shard_map/while/body/eval_jaxpr/psum | solution.py:160
  1121.3 43.3 %all-gather.5.cloned.1.call-done = bf16[32,4,8192]{2,1,0:T(4,128)(2,1)} async-done(((bf16[1,4,8192]{2,1,0:T(4,128)(2,1)}), bf16[32,4,8192]{2,1,0:T(4,128)(2,1)}) %all-gather.5.cloned.1.call-update) | async-done | bytes 2097168 | tf_op jit(solution)/shard_map/while/body/eval_jaxpr/all_gather | solution.py:125
  1196.8 11.0 all_to_all.139
  1212.1 105.2 %all-reduce.9.cloned.1.call-done = bf16[128,8192]{1,0:T(8,128)(2,1)} async-done(((bf16[128,8192]{1,0:T(8,128)(2,1)}), bf16[128,8192]{1,0:T(8,128)(2,1)}) %all-reduce.9.cloned.1.call-update) | async-done | bytes 2097168 | tf_op jit(solution)/shard_map/while/body/eval_jaxpr/psum | solution.py:160
  1329.6 43.3 %all-gather.5.cloned.1.call-done = bf16[32,4,8192]{2,1,0:T(4,128)(2,1)} async-done(((bf16[1,4,8192]{2,1,0:T(4,128)(2,1)}), bf16[32,4,8192]{2,1,0:T(4,128)(2,1)}) %all-gather.5.cloned.1.call-update) | async-done | bytes 2097168 | tf_op jit(solution)/shard_map/while/body/eval_jaxpr/all_gather | solution.py:125
  1405.1 11.0 all_to_all.139
  1420.4 105.3 %all-reduce.9.cloned.1.call-done = bf16[128,8192]{1,0:T(8,128)(2,1)} async-done(((bf16[128,8192]{1,0:T(8,128)(2,1)}), bf16[128,8192]{1,0:T(8,128)(2,1)}) %all-reduce.9.cloned.1.call-update) | async-done | bytes 2097168 | tf_op jit(solution)/shard_map/while/body/eval_jaxpr/psum | solution.py:160
  1535.3 44.9 %all-reduce.7.cloned.1.call-done = f32[4,4,8192]{2,1,0:T(4,128)} async-done(((f32[4,4,8192]{2,1,0:T(4,128)}), f32[4,4,8192]{2,1,0:T(4,128)}) %all-reduce.7.cloned.1.call-update) | async-done | bytes 524304
  (595 shorter events, 368.8 us)
Async XLA Ops:
  6.5 53.0 %all-reduce.5.cloned.1.call-start = ((), (), s32[]{:S(2)}) async-start(), calls=%async_computation.4 | async-start | bytes 524288 | tf_op jit(solution)/shard_map/psum | solution.py:100
  59.5 16.1 %all-to-all-start.3 = ((bf16[4,128,256]{2,0,1:T(4,128)(2,1)}), bf16[4,128,256]{2,0,1:T(4,128)(2,1)S(1)}, u32[]{:S(2)}, u32[]{:S(2)}) async-start(bf16[4,128,256]{2,0,1:T(4,128)(2,1)} %all-reduce.5.cloned.1.call-done), calls=%async_computation.3 | async-start | bytes 524288 | tf_op jit(solution)/shard_map/all_to_all | solution.py:101
  76.9 45.9 %all-gather.5.cloned.1.call-start = ((), (), s32[]{:S(2)}) async-start(), calls=%async_computation.6 | async-start | bytes 2162688 | tf_op jit(solution)/shard_map/while/body/eval_jaxpr/all_gather | solution.py:125
  128.3 12.6 all-to-all-start.1
  144.9 130.6 %all-reduce.9.cloned.1.call-start = ((), (), s32[]{:S(2)}) async-start(), calls=%async_computation.7 | async-start | bytes 4194304 | tf_op jit(solution)/shard_map/while/body/eval_jaxpr/psum | solution.py:160
  283.4 47.8 %all-gather.5.cloned.1.call-start = ((), (), s32[]{:S(2)}) async-start(), calls=%async_computation.6 | async-start | bytes 2162688 | tf_op jit(solution)/shard_map/while/body/eval_jaxpr/all_gather | solution.py:125
  336.7 12.6 all-to-all-start.1
  353.2 130.6 %all-reduce.9.cloned.1.call-start = ((), (), s32[]{:S(2)}) async-start(), calls=%async_computation.7 | async-start | bytes 4194304 | tf_op jit(solution)/shard_map/while/body/eval_jaxpr/psum | solution.py:160
  491.7 47.8 %all-gather.5.cloned.1.call-start = ((), (), s32[]{:S(2)}) async-start(), calls=%async_computation.6 | async-start | bytes 2162688 | tf_op jit(solution)/shard_map/while/body/eval_jaxpr/all_gather | solution.py:125
  545.0 12.6 all-to-all-start.1
  561.5 130.6 %all-reduce.9.cloned.1.call-start = ((), (), s32[]{:S(2)}) async-start(), calls=%async_computation.7 | async-start | bytes 4194304 | tf_op jit(solution)/shard_map/while/body/eval_jaxpr/psum | solution.py:160
  700.0 48.1 %all-gather.5.cloned.1.call-start = ((), (), s32[]{:S(2)}) async-start(), calls=%async_computation.6 | async-start | bytes 2162688 | tf_op jit(solution)/shard_map/while/body/eval_jaxpr/all_gather | solution.py:125
  753.6 12.6 all-to-all-start.1
  770.1 130.6 %all-reduce.9.cloned.1.call-start = ((), (), s32[]{:S(2)}) async-start(), calls=%async_computation.7 | async-start | bytes 4194304 | tf_op jit(solution)/shard_map/while/body/eval_jaxpr/psum | solution.py:160
  908.6 47.8 %all-gather.5.cloned.1.call-start = ((), (), s32[]{:S(2)}) async-start(), calls=%async_computation.6 | async-start | bytes 2162688 | tf_op jit(solution)/shard_map/while/body/eval_jaxpr/all_gather | solution.py:125
  961.9 12.6 all-to-all-start.1
  978.4 130.6 %all-reduce.9.cloned.1.call-start = ((), (), s32[]{:S(2)}) async-start(), calls=%async_computation.7 | async-start | bytes 4194304 | tf_op jit(solution)/shard_map/while/body/eval_jaxpr/psum | solution.py:160
  1116.9 47.8 %all-gather.5.cloned.1.call-start = ((), (), s32[]{:S(2)}) async-start(), calls=%async_computation.6 | async-start | bytes 2162688 | tf_op jit(solution)/shard_map/while/body/eval_jaxpr/all_gather | solution.py:125
  1170.2 12.6 all-to-all-start.1
  1186.7 130.6 %all-reduce.9.cloned.1.call-start = ((), (), s32[]{:S(2)}) async-start(), calls=%async_computation.7 | async-start | bytes 4194304 | tf_op jit(solution)/shard_map/while/body/eval_jaxpr/psum | solution.py:160
  1325.2 47.8 %all-gather.5.cloned.1.call-start = ((), (), s32[]{:S(2)}) async-start(), calls=%async_computation.6 | async-start | bytes 2162688 | tf_op jit(solution)/shard_map/while/body/eval_jaxpr/all_gather | solution.py:125
  1378.5 12.6 all-to-all-start.1
  1395.0 130.6 %all-reduce.9.cloned.1.call-start = ((), (), s32[]{:S(2)}) async-start(), calls=%async_computation.7 | async-start | bytes 4194304 | tf_op jit(solution)/shard_map/while/body/eval_jaxpr/psum | solution.py:160
  1533.5 46.7 %all-reduce.7.cloned.1.call-start = ((), (), s32[]{:S(2)}) async-start(), calls=%async_computation.5 | async-start | bytes 1048576
  (94 other events, 3158.5 us)
Sparse Core Ops, SparseCore 0:
  15.4 44.1 all-reduce.4
  80.3 42.4 all-gather.4
  170.4 105.0 all-reduce.8
  286.4 44.6 all-gather.4
  378.7 105.0 all-reduce.8
  494.7 44.6 all-gather.4
  587.0 105.0 all-reduce.8
  703.3 44.6 all-gather.4
  795.6 105.0 all-reduce.8
  911.6 44.6 all-gather.4
  1003.9 105.0 all-reduce.8
  1119.9 44.6 all-gather.4
  1212.2 105.0 all-reduce.8
  1328.2 44.6 all-gather.4
  1420.5 105.0 all-reduce.8
  1536.5 43.7 all-reduce.6
where the time goes:
time: 1590 us
  waiting for transfers between devices  1210 us (76%)
  starting transfers between devices  95.2 us (6%)
  matrix products  77.1 us (5%)
  blocking collectives  76.7 us (5%)
  local copies, waits for them, and re-layouts  60.2 us (4%)
  other arithmetic  50.7 us (3%)
    psum x7, waiting for transfers between devices, advance(): lax.psum(partial_value.astype(jnp.bfloat16), 'tensor').astype(jnp.float32)  737 us
    all_gather x7, waiting for transfers between devices, advance(): lax.all_gather(normalize(hidden_in, gain_vec), 'tensor', axis=0, tiled=True)  302 us
    all_to_all x7, blocking collectives, advance(): lax.all_to_all(mixed_out, 'tensor', split_axis=1, concat_axis=0, tiled=True)  76.7 us
    unnamed x3, waiting for transfers between devices  45.4 us
    psum x1, waiting for transfers between devices, body(): columns = lax.psum(partial_embed.astype(jnp.bfloat16), 'section')  44.3 us
    all_to_all x7, waiting for transfers between devices, advance(): lax.all_to_all(queries, 'tensor', split_axis=0, concat_axis=1, tiled=True)  37.2 us
    all_to_all x7, starting transfers between devices, advance(): lax.all_to_all(keyvals, 'tensor', split_axis=0, concat_axis=1, tiled=True)  36.6 us
  transfers between devices with their start and end apart: 38, of which 38 were waited for; matrix products, arithmetic and copies ran while one was open for 4% of the time, Pallas kernels for 0%

commit v1 on v0

--- a/solution.py
+++ b/solution.py
@@ -122,7 +122,9 @@
         step_embed = lax.dynamic_index_in_dim(own_embed, step_index, 0, keepdims=False)
         first_input = step_embed.astype(jnp.float32)
         hidden_in = jnp.where(section_pos == 0, first_input, incoming)
-        normed = lax.all_gather(normalize(hidden_in, gain_vec), "tensor", axis=0, tiled=True)
+        block_2 = normalize(hidden_in, gain_vec)
+        repeated = jnp.stack([block_2] * lax.axis_size("tensor"))
+        normed = jnp.concatenate(lax.all_to_all(repeated, "tensor", 0, 0), axis=0)
         queries = jnp.dot(normed, query_mat, preferred_element_type=jnp.float32)
         keyvals = jnp.dot(normed, keyval_mat, preferred_element_type=jnp.float32)
         queries, keyvals = (

time: 1590 us -> 1530 us (0.962)
  waiting for transfers between devices: 1210 us -> 1100 us
  starting transfers between devices: 95.2 us -> 134 us
  matrix products: 77.1 us -> 106 us
    all_gather x7 -> x0, waiting for transfers between devices: 302 us -> none  [advance(): lax.all_gather(normalize(hidden_in, gain_vec), 'tensor', axis=0, tiled=True)]
    all_to_all x0 -> x7, waiting for transfers between devices: none -> 188 us  [advance(): normed = jnp.concatenate(lax.all_to_all(repeated, 'tensor', 0, 0), axis=0)]
    all_to_all x0 -> x7, starting transfers between devices: none -> 39.6 us  [advance(): normed = jnp.concatenate(lax.all_to_all(repeated, 'tensor', 0, 0), axis=0)]
    while x196 -> x77, local copies, waits for them, and re-layouts: 23.7 us -> 5.73 us
  transfers between devices with their start and end apart: 38 -> 38, of which waited for: 38 -> 38; matrix products, arithmetic and copies ran while one was open for 4% -> 5% of each run, Pallas kernels for 0% -> 0%
where the time goes in v1:
time: 1530 us
  waiting for transfers between devices  1100 us (72%)
  starting transfers between devices  134 us (9%)
  matrix products  106 us (7%)
  blocking collectives  76.7 us (5%)
  local copies, waits for them, and re-layouts  64.2 us (4%)
  other arithmetic  35.7 us (2%)
    psum x7, waiting for transfers between devices, advance(): lax.psum(partial_value.astype(jnp.bfloat16), 'tensor').astype(jnp.float32)  742 us
    all_to_all x7, waiting for transfers between devices, advance(): normed = jnp.concatenate(lax.all_to_all(repeated, 'tensor', 0, 0), axis=0)  188 us
    all_to_all x7, blocking collectives, advance(): lax.all_to_all(mixed_out, 'tensor', split_axis=1, concat_axis=0, tiled=True)  76.7 us
    unnamed x3, waiting for transfers between devices  45 us
    psum x1, waiting for transfers between devices, body(): columns = lax.psum(partial_embed.astype(jnp.bfloat16), 'section')  44.3 us
    all_to_all x7, starting transfers between devices, advance(): normed = jnp.concatenate(lax.all_to_all(repeated, 'tensor', 0, 0), axis=0)  39.6 us
    all_to_all x7, waiting for transfers between devices, advance(): lax.all_to_all(queries, 'tensor', split_axis=0, concat_axis=1, tiled=True)  37.6 us
    all_to_all x7, starting transfers between devices, advance(): lax.all_to_all(queries, 'tensor', split_axis=0, concat_axis=1, tiled=True)  36.4 us
  transfers between devices with their start and end apart: 38, of which 38 were waited for; matrix products, arithmetic and copies ran while one was open for 5% of the time, Pallas kernels for 0%

profile of v1, /device:TPU:0, one launch (start us, length us, event | category | flops | bytes accessed | tf_op | source)
XLA Modules:
  0.0 1527.8 jit_solution(15455138357165563362)
XLA Ops:
  15.4 44.3 %all-reduce.5.cloned.1.call-done = bf16[4,128,256]{2,0,1:T(4,128)(2,1)} async-done(((bf16[4,128,256]{2,0,1:T(4,128)(2,1)}), bf16[4,128,256]{2,0,1:T(4,128)(2,1)}) %all-reduce.5.cloned.1.call-update) | async-done | bytes 262160 | tf_op jit(solution)/shard_map/psum | solution.py:100
  76.2 1395.9 %while.19 = (s32[]{:T(128)}, f32[4,8192]{1,0:T(4,128)S(1)}, bf16[4,4,2,1024]{3,1,2,0:T(4,128)(2,1)S(1)}, f32[4,4,8192]{2,1,0:T(4,128)S(1)}, pred[]{:T(512)}, /*i...) while((s32[]{:T(128)}, f32[4,8192]{1,0:T(4,128)S(1)}, ...), condition=%wide.region_8.9_spmd, body=%wide.region_1.8_spmd.sunk | while | flops 1228397952 | bytes 49518836 | solution.py:177
  86.7 26.8 %all-to-all-done = bf16[32,4,8192]{2,1,0:T(4,128)(2,1)} async-done(((bf16[32,4,8192]{2,1,0:T(4,128)(2,1)}), bf16[32,4,8192]{2,1,0:T(4,128)(2,1)}, u32[]{:S(2)}, u32[]{:S(2)}) %all-to-all-start) | async-done | bytes 2097184 | tf_op jit(solution)/shard_map/while/body/eval_jaxpr/all_to_all | solution.py:127
  146.4 11.0 all_to_all.146
  161.7 104.5 %all-reduce.9.cloned.1.call-done = bf16[128,8192]{1,0:T(8,128)(2,1)} async-done(((bf16[128,8192]{1,0:T(8,128)(2,1)}), bf16[128,8192]{1,0:T(8,128)(2,1)}) %all-reduce.9.cloned.1.call-update) | async-done | bytes 2097168 | tf_op jit(solution)/shard_map/while/body/eval_jaxpr/psum | solution.py:162
  284.7 26.9 %all-to-all-done = bf16[32,4,8192]{2,1,0:T(4,128)(2,1)} async-done(((bf16[32,4,8192]{2,1,0:T(4,128)(2,1)}), bf16[32,4,8192]{2,1,0:T(4,128)(2,1)}, u32[]{:S(2)}, u32[]{:S(2)}) %all-to-all-start) | async-done | bytes 2097184 | tf_op jit(solution)/shard_map/while/body/eval_jaxpr/all_to_all | solution.py:127
  344.4 11.0 all_to_all.146
  359.7 106.2 %all-reduce.9.cloned.1.call-done = bf16[128,8192]{1,0:T(8,128)(2,1)} async-done(((bf16[128,8192]{1,0:T(8,128)(2,1)}), bf16[128,8192]{1,0:T(8,128)(2,1)}) %all-reduce.9.cloned.1.call-update) | async-done | bytes 2097168 | tf_op jit(solution)/shard_map/while/body/eval_jaxpr/psum | solution.py:162
  484.6 26.9 %all-to-all-done = bf16[32,4,8192]{2,1,0:T(4,128)(2,1)} async-done(((bf16[32,4,8192]{2,1,0:T(4,128)(2,1)}), bf16[32,4,8192]{2,1,0:T(4,128)(2,1)}, u32[]{:S(2)}, u32[]{:S(2)}) %all-to-all-start) | async-done | bytes 2097184 | tf_op jit(solution)/shard_map/while/body/eval_jaxpr/all_to_all | solution.py:127
  544.3 11.0 all_to_all.146
  559.5 106.2 %all-reduce.9.cloned.1.call-done = bf16[128,8192]{1,0:T(8,128)(2,1)} async-done(((bf16[128,8192]{1,0:T(8,128)(2,1)}), bf16[128,8192]{1,0:T(8,128)(2,1)}) %all-reduce.9.cloned.1.call-update) | async-done | bytes 2097168 | tf_op jit(solution)/shard_map/while/body/eval_jaxpr/psum | solution.py:162
  684.4 26.9 %all-to-all-done = bf16[32,4,8192]{2,1,0:T(4,128)(2,1)} async-done(((bf16[32,4,8192]{2,1,0:T(4,128)(2,1)}), bf16[32,4,8192]{2,1,0:T(4,128)(2,1)}, u32[]{:S(2)}, u32[]{:S(2)}) %all-to-all-start) | async-done | bytes 2097184 | tf_op jit(solution)/shard_map/while/body/eval_jaxpr/all_to_all | solution.py:127
  744.1 11.0 all_to_all.146
  759.3 106.2 %all-reduce.9.cloned.1.call-done = bf16[128,8192]{1,0:T(8,128)(2,1)} async-done(((bf16[128,8192]{1,0:T(8,128)(2,1)}), bf16[128,8192]{1,0:T(8,128)(2,1)}) %all-reduce.9.cloned.1.call-update) | async-done | bytes 2097168 | tf_op jit(solution)/shard_map/while/body/eval_jaxpr/psum | solution.py:162
  884.2 26.9 %all-to-all-done = bf16[32,4,8192]{2,1,0:T(4,128)(2,1)} async-done(((bf16[32,4,8192]{2,1,0:T(4,128)(2,1)}), bf16[32,4,8192]{2,1,0:T(4,128)(2,1)}, u32[]{:S(2)}, u32[]{:S(2)}) %all-to-all-start) | async-done | bytes 2097184 | tf_op jit(solution)/shard_map/while/body/eval_jaxpr/all_to_all | solution.py:127
  943.9 11.0 all_to_all.146
  959.1 106.2 %all-reduce.9.cloned.1.call-done = bf16[128,8192]{1,0:T(8,128)(2,1)} async-done(((bf16[128,8192]{1,0:T(8,128)(2,1)}), bf16[128,8192]{1,0:T(8,128)(2,1)}) %all-reduce.9.cloned.1.call-update) | async-done | bytes 2097168 | tf_op jit(solution)/shard_map/while/body/eval_jaxpr/psum | solution.py:162
  1084.0 26.9 %all-to-all-done = bf16[32,4,8192]{2,1,0:T(4,128)(2,1)} async-done(((bf16[32,4,8192]{2,1,0:T(4,128)(2,1)}), bf16[32,4,8192]{2,1,0:T(4,128)(2,1)}, u32[]{:S(2)}, u32[]{:S(2)}) %all-to-all-start) | async-done | bytes 2097184 | tf_op jit(solution)/shard_map/while/body/eval_jaxpr/all_to_all | solution.py:127
  1143.7 11.0 all_to_all.146
  1158.9 106.2 %all-reduce.9.cloned.1.call-done = bf16[128,8192]{1,0:T(8,128)(2,1)} async-done(((bf16[128,8192]{1,0:T(8,128)(2,1)}), bf16[128,8192]{1,0:T(8,128)(2,1)}) %all-reduce.9.cloned.1.call-update) | async-done | bytes 2097168 | tf_op jit(solution)/shard_map/while/body/eval_jaxpr/psum | solution.py:162
  1283.8 26.9 %all-to-all-done = bf16[32,4,8192]{2,1,0:T(4,128)(2,1)} async-done(((bf16[32,4,8192]{2,1,0:T(4,128)(2,1)}), bf16[32,4,8192]{2,1,0:T(4,128)(2,1)}, u32[]{:S(2)}, u32[]{:S(2)}) %all-to-all-start) | async-done | bytes 2097184 | tf_op jit(solution)/shard_map/while/body/eval_jaxpr/all_to_all | solution.py:127
  1343.5 11.0 all_to_all.146
  1358.8 106.2 %all-reduce.9.cloned.1.call-done = bf16[128,8192]{1,0:T(8,128)(2,1)} async-done(((bf16[128,8192]{1,0:T(8,128)(2,1)}), bf16[128,8192]{1,0:T(8,128)(2,1)}) %all-reduce.9.cloned.1.call-update) | async-done | bytes 2097168 | tf_op jit(solution)/shard_map/while/body/eval_jaxpr/psum | solution.py:162
  1474.2 44.9 %all-reduce.7.cloned.1.call-done = f32[4,4,8192]{2,1,0:T(4,128)} async-done(((f32[4,4,8192]{2,1,0:T(4,128)}), f32[4,4,8192]{2,1,0:T(4,128)}) %all-reduce.7.cloned.1.call-update) | async-done | bytes 524304
  (484 shorter events, 417.0 us)
Async XLA Ops:
  6.5 53.1 %all-reduce.5.cloned.1.call-start = ((), (), s32[]{:S(2)}) async-start(), calls=%async_computation.5 | async-start | bytes 524288 | tf_op jit(solution)/shard_map/psum | solution.py:100
  59.7 16.1 %all-to-all-start.4 = ((bf16[4,128,256]{2,0,1:T(4,128)(2,1)}), bf16[4,128,256]{2,0,1:T(4,128)(2,1)S(1)}, u32[]{:S(2)}, u32[]{:S(2)}) async-start(bf16[4,128,256]{2,0,1:T(4,128)(2,1)} %all-reduce.5.cloned.1.call-done), calls=%async_computation.4 | async-start | bytes 524288 | tf_op jit(solution)/shard_map/all_to_all | solution.py:101
  78.8 34.7 %all-to-all-start = ((bf16[32,4,8192]{2,1,0:T(4,128)(2,1)}), bf16[32,4,8192]{2,1,0:T(4,128)(2,1)}, u32[]{:S(2)}, u32[]{:S(2)}) async-start(bf16[32,4,8192]{2,1,0:T(4,128)(2,1)} %stack.25), calls=%async_computation | async-start | bytes 4194304 | tf_op jit(solution)/shard_map/while/body/eval_jaxpr/all_to_all | solution.py:127
  129.0 13.0 all-to-all-start.1
  134.2 131.9 %all-reduce.9.cloned.1.call-start = ((), (), s32[]{:S(2)}) async-start(), calls=%async_computation.7 | async-start | bytes 4194304 | tf_op jit(solution)/shard_map/while/body/eval_jaxpr/psum | solution.py:162
  275.8 35.8 %all-to-all-start = ((bf16[32,4,8192]{2,1,0:T(4,128)(2,1)}), bf16[32,4,8192]{2,1,0:T(4,128)(2,1)}, u32[]{:S(2)}, u32[]{:S(2)}) async-start(bf16[32,4,8192]{2,1,0:T(4,128)(2,1)} %stack.25), calls=%async_computation | async-start | bytes 4194304 | tf_op jit(solution)/shard_map/while/body/eval_jaxpr/all_to_all | solution.py:127
  327.1 13.0 all-to-all-start.1
  332.3 133.7 %all-reduce.9.cloned.1.call-start = ((), (), s32[]{:S(2)}) async-start(), calls=%async_computation.7 | async-start | bytes 4194304 | tf_op jit(solution)/shard_map/while/body/eval_jaxpr/psum | solution.py:162
  475.6 35.8 %all-to-all-start = ((bf16[32,4,8192]{2,1,0:T(4,128)(2,1)}), bf16[32,4,8192]{2,1,0:T(4,128)(2,1)}, u32[]{:S(2)}, u32[]{:S(2)}) async-start(bf16[32,4,8192]{2,1,0:T(4,128)(2,1)} %stack.25), calls=%async_computation | async-start | bytes 4194304 | tf_op jit(solution)/shard_map/while/body/eval_jaxpr/all_to_all | solution.py:127
  526.9 13.0 all-to-all-start.1
  532.1 133.7 %all-reduce.9.cloned.1.call-start = ((), (), s32[]{:S(2)}) async-start(), calls=%async_computation.7 | async-start | bytes 4194304 | tf_op jit(solution)/shard_map/while/body/eval_jaxpr/psum | solution.py:162
  675.5 35.8 %all-to-all-start = ((bf16[32,4,8192]{2,1,0:T(4,128)(2,1)}), bf16[32,4,8192]{2,1,0:T(4,128)(2,1)}, u32[]{:S(2)}, u32[]{:S(2)}) async-start(bf16[32,4,8192]{2,1,0:T(4,128)(2,1)} %stack.25), calls=%async_computation | async-start | bytes 4194304 | tf_op jit(solution)/shard_map/while/body/eval_jaxpr/all_to_all | solution.py:127
  726.7 13.0 all-to-all-start.1
  731.9 133.7 %all-reduce.9.cloned.1.call-start = ((), (), s32[]{:S(2)}) async-start(), calls=%async_computation.7 | async-start | bytes 4194304 | tf_op jit(solution)/shard_map/while/body/eval_jaxpr/psum | solution.py:162
  875.3 35.8 %all-to-all-start = ((bf16[32,4,8192]{2,1,0:T(4,128)(2,1)}), bf16[32,4,8192]{2,1,0:T(4,128)(2,1)}, u32[]{:S(2)}, u32[]{:S(2)}) async-start(bf16[32,4,8192]{2,1,0:T(4,128)(2,1)} %stack.25), calls=%async_computation | async-start | bytes 4194304 | tf_op jit(solution)/shard_map/while/body/eval_jaxpr/all_to_all | solution.py:127
  926.5 13.0 all-to-all-start.1
  931.7 133.7 %all-reduce.9.cloned.1.call-start = ((), (), s32[]{:S(2)}) async-start(), calls=%async_computation.7 | async-start | bytes 4194304 | tf_op jit(solution)/shard_map/while/body/eval_jaxpr/psum | solution.py:162
  1075.1 35.8 %all-to-all-start = ((bf16[32,4,8192]{2,1,0:T(4,128)(2,1)}), bf16[32,4,8192]{2,1,0:T(4,128)(2,1)}, u32[]{:S(2)}, u32[]{:S(2)}) async-start(bf16[32,4,8192]{2,1,0:T(4,128)(2,1)} %stack.25), calls=%async_computation | async-start | bytes 4194304 | tf_op jit(solution)/shard_map/while/body/eval_jaxpr/all_to_all | solution.py:127
  1126.3 13.0 all-to-all-start.1
  1131.5 133.7 %all-reduce.9.cloned.1.call-start = ((), (), s32[]{:S(2)}) async-start(), calls=%async_computation.7 | async-start | bytes 4194304 | tf_op jit(solution)/shard_map/while/body/eval_jaxpr/psum | solution.py:162
  1274.9 35.8 %all-to-all-start = ((bf16[32,4,8192]{2,1,0:T(4,128)(2,1)}), bf16[32,4,8192]{2,1,0:T(4,128)(2,1)}, u32[]{:S(2)}, u32[]{:S(2)}) async-start(bf16[32,4,8192]{2,1,0:T(4,128)(2,1)} %stack.25), calls=%async_computation | async-start | bytes 4194304 | tf_op jit(solution)/shard_map/while/body/eval_jaxpr/all_to_all | solution.py:127
  1326.1 13.0 all-to-all-start.1
  1331.3 133.7 %all-reduce.9.cloned.1.call-start = ((), (), s32[]{:S(2)}) async-start(), calls=%async_computation.7 | async-start | bytes 4194304 | tf_op jit(solution)/shard_map/while/body/eval_jaxpr/psum | solution.py:162
  1472.1 47.0 %all-reduce.7.cloned.1.call-start = ((), (), s32[]{:S(2)}) async-start(), calls=%async_computation.6 | async-start | bytes 1048576
  (39 other events, 1358.5 us)
Sparse Core Ops, SparseCore 0:
  15.5 44.1 all-reduce.4
  161.8 104.2 all-reduce.8
  359.8 106.0 all-reduce.8
  559.6 106.0 all-reduce.8
  759.4 106.0 all-reduce.8
  959.2 106.0 all-reduce.8
  1159.1 106.0 all-reduce.8
  1358.9 106.0 all-reduce.8
  1475.4 43.6 all-reduce.6
